TPU v7x, 1024 devices: a whole 4x4x32 slice. The times are simulated.
1024 devices in a mesh: expert: 32 (over z_lo, core), fsdp: 4 (over x), dp: 8 (over z_hi, y).
Axes of the slice: x: 4, y: 4, z: 32 (z_hi: 2, z_lo: 16; z = z_hi * 16 + z_lo), core: 2. Of those that a mesh axis runs over, the one named last changes fastest.
Arguments:
- tokens: bfloat16 [131072, 1664], P(('expert', 'fsdp', 'dp')), may hold values from -6 to 6
- grad_out: bfloat16 [131072, 1664], P(('expert', 'fsdp', 'dp')), may hold values from -0.29882812 to 0.29882812
- slot_token: int32 [1024, 32, 2], P(('expert', 'fsdp', 'dp')), may hold values from 0 to 127
- slot_gate: float32 [1024, 32, 2], P(('expert', 'fsdp', 'dp')), may hold values from 0.1 to 1
- w_in: bfloat16 [32, 4096, 1664], P('expert', 'fsdp'), may hold values from -0.15625 to 0.15625
- w_out: bfloat16 [32, 4096, 1664], P('expert', 'fsdp'), may hold values from -0.09375 to 0.09375
Outputs:
- mixed: bfloat16 [131072, 1664], P(('expert', 'fsdp', 'dp'))
- weight_grad: float32 [32, 4096, 1664], P('expert', ('fsdp', 'dp'))
Inputs may be any that keep to these rules, and one draw needn't show every extreme that they name: `slot_token`: each slot names a token of its own shard; a token may fill several slots or none.
All inputs are finite; a program needn't handle non-finite values.
Results may differ from a plain program's by a relative error of at most 0.017.
Values may be sent and summed in bfloat16 or wider, within the bound.
A program may use at most 64 MiB of HBM per device.

v0:
```python
import jax
import jax.numpy as jnp
from jax import lax
from jax.sharding import PartitionSpec as P


def gelu_parts(value):
    normal_cdf = 0.5 * (1.0 + jax.scipy.special.erf(value * 0.7071067811865476))
    normal_pdf = jnp.exp(-0.5 * value * value) * 0.3989422804014327
    return (value * normal_cdf, normal_cdf + value * normal_pdf)


def body(tokens, grad_out, slot_token, slot_gate, w_in, w_out):
    experts = slot_token.shape[1]
    capacity = slot_token.shape[2]
    tok_count = tokens.shape[0]
    width = tokens.shape[1]
    slots = experts * capacity
    picked = slot_token.reshape(slots, 1) == jnp.arange(tok_count, dtype=jnp.int32)[None, :]
    pick_mat = picked.astype(jnp.bfloat16)
    gate_col = slot_gate.reshape(slots, 1)
    slot_in = jnp.dot(pick_mat, tokens, preferred_element_type=jnp.float32).astype(jnp.bfloat16)
    slot_grad = (jnp.dot(pick_mat, grad_out, preferred_element_type=jnp.float32) * gate_col).astype(
        jnp.bfloat16
    )
    slot_in = slot_in.reshape(experts, capacity, width)
    slot_grad = slot_grad.reshape(experts, capacity, width)
    weight_in = w_in[0]
    weight_out = w_out[0]
    arrived = (
        lax.all_to_all(slot_in, "expert", split_axis=0, concat_axis=0, tiled=True),
        lax.all_to_all(slot_grad, "expert", split_axis=0, concat_axis=0, tiled=True),
    )
    x_mine = arrived[0].reshape(slots, width)
    g_mine = arrived[1].reshape(slots, width)
    x_rows = lax.all_gather(x_mine, "fsdp", axis=0, tiled=True)
    g_rows = lax.all_gather(g_mine, "fsdp", axis=0, tiled=True)
    pre = lax.dot_general(
        x_rows, weight_in, (((1,), (1,)), ((), ())), preferred_element_type=jnp.float32
    )
    act_value, slope = gelu_parts(pre)
    act = act_value.astype(jnp.bfloat16)
    partial_value = jnp.dot(act, weight_out, preferred_element_type=jnp.float32)
    back = lax.dot_general(
        g_rows, weight_out, (((1,), (1,)), ((), ())), preferred_element_type=jnp.float32
    )
    dpre = (back * slope).astype(jnp.bfloat16)
    out_buf = partial_value
    dpre_buf = dpre
    x_buf = x_rows
    out_buf, dpre_buf, x_buf = (out_buf, dpre_buf, x_buf)
    summed = lax.psum_scatter(out_buf.astype(jnp.bfloat16), "fsdp", scatter_dimension=0, tiled=True)
    expert_out = summed.reshape(experts, capacity, width)
    returned = lax.all_to_all(expert_out, "expert", split_axis=0, concat_axis=0, tiled=True)
    combine = picked.astype(jnp.float32) * gate_col
    mixed = lax.dot_general(
        combine,
        returned.reshape(slots, width).astype(jnp.float32),
        (((0,), (0,)), ((), ())),
        precision=lax.Precision.HIGHEST,
        preferred_element_type=jnp.float32,
    ).astype(jnp.bfloat16)
    term = lax.dot_general(
        dpre_buf, x_buf, (((0,), (0,)), ((), ())), preferred_element_type=jnp.float32
    )
    weight_grad = lax.psum_scatter(
        term.astype(jnp.bfloat16), "dp", scatter_dimension=0, tiled=True
    ).astype(jnp.float32)
    return (mixed, weight_grad[None])


def solution(mesh):
    placed = (
        P(("expert", "fsdp", "dp"), None),
        P(("expert", "fsdp", "dp"), None),
        P(("expert", "fsdp", "dp"), None, None),
        P(("expert", "fsdp", "dp"), None, None),
        P("expert", "fsdp", None),
        P("expert", "fsdp", None),
    )
    return jax.shard_map(
        body,
        mesh=mesh,
        in_specs=placed,
        out_specs=(P(("expert", "fsdp", "dp"), None), P("expert", ("fsdp", "dp"), None)),
        check_vma=False,
    )
```

profile of v0, /device:TPU:6, one launch (start us, length us, event | category | flops | bytes accessed | tf_op | source)
XLA Modules:
  0.0 483.2 jit_solution(3047081219797767670)
XLA Ops:
  7.2 0.0 copy-start
  7.2 0.9 copy.10
  8.1 0.1 eq.15
  8.2 2.0 convolution_convert_fusion.2
  10.2 1.7 reshape.26
  11.9 26.3 %all-to-all-start = ((bf16[32,2,1664]{2,1,0:T(2,128)(2,1)}), bf16[32,2,1664]{2,1,0:T(2,128)(2,1)}, u32[]{:S(2)}, u32[]{:S(2)}) async-start(bf16[32,2,1664]{2,1,0:T(2,128)(2,1)} %reshape.26), calls=%async_computation | async-start | bytes 425984 | tf_op jit(solution)/shard_map/all_to_all | solution.py:31
  38.1 0.8 copy.11
  38.9 0.1 mul.54
  39.0 2.0 fusion.9
  41.0 1.7 reshape.30
  42.7 25.5 %all-to-all-done = bf16[32,2,1664]{2,1,0:T(2,128)(2,1)} async-done(((bf16[32,2,1664]{2,1,0:T(2,128)(2,1)}), bf16[32,2,1664]{2,1,0:T(2,128)(2,1)}, u32[]{:S(2)}, u32[]{:S(2)}) %all-to-all-start) | async-done | bytes 213024 | tf_op jit(solution)/shard_map/all_to_all | solution.py:31
  68.1 9.6 %all-to-all-start.2 = ((bf16[32,2,1664]{2,1,0:T(2,128)(2,1)}), bf16[32,2,1664]{2,1,0:T(2,128)(2,1)}, u32[]{:S(2)}, u32[]{:S(2)}) async-start(bf16[32,2,1664]{2,1,0:T(2,128)(2,1)} %reshape.30), calls=%async_computation.3 | async-start | bytes 425984 | tf_op jit(solution)/shard_map/all_to_all | solution.py:32
  77.7 0.0 reduce-scatter.3.cloned.1.call-start
  77.8 1.7 reshape.27
  79.5 14.6 %all_gather.6 = bf16[256,1664]{1,0:T(8,128)(2,1)S(1)} all-gather(bf16[64,1664]{1,0:T(8,128)(2,1)} %reshape.27), channel_id=1, replica_groups=mesh['expert'=32,'fsdp'=4,'dp'=8] {'fsdp'}, dimensions={0}, use_global_device_ids=true | all-gather | bytes 1064960 | tf_op jit(solution)/shard_map/all_gather | solution.py:36
  94.0 0.0 copy-start.1
  94.0 0.9 copy-done.1
  94.9 3.1 fusion.4
  98.1 0.0 copy-start.2
  98.1 1.0 copy-done.2
  99.0 0.0 copy-done
  99.0 2.0 fusion.6
  101.1 0.0 reduce-scatter.3.cloned.1.call-update
  101.1 0.0 reduce-scatter.5.cloned.1.call-start
  101.1 6.6 %all-to-all-done.2 = bf16[32,2,1664]{2,1,0:T(2,128)(2,1)} async-done(((bf16[32,2,1664]{2,1,0:T(2,128)(2,1)}), bf16[32,2,1664]{2,1,0:T(2,128)(2,1)}, u32[]{:S(2)}, u32[]{:S(2)}) %all-to-all-start.2) | async-done | bytes 213024 | tf_op jit(solution)/shard_map/all_to_all | solution.py:32
  107.7 1.7 reshape.31
  109.4 14.7 %all_gather.7 = bf16[256,1664]{1,0:T(8,128)(2,1)} all-gather(bf16[64,1664]{1,0:T(8,128)(2,1)} %reshape.31), channel_id=1, replica_groups=mesh['expert'=32,'fsdp'=4,'dp'=8] {'fsdp'}, dimensions={0}, use_global_device_ids=true | all-gather | bytes 1064960 | tf_op jit(solution)/shard_map/all_gather | solution.py:37
  124.1 5.8 %convolution_convert_fusion = bf16[1024,1664]{1,0:T(8,128)(2,1)} fusion(bf16[256,1664]{1,0:T(8,128)(2,1)} %copy-done.1, bf16[256,1664]{1,0:T(8,128)(2,1)} %all_gather.7, bf16[1,1024,1664]{2,1,0:T(8,128)(2,1)S(1)} %copy-done, f32[256,1024]{1,0:T(8,128)} %copy-done.2), kind=kOutput, calls=%fused_computation | convolution fusion | flops 1749155840 | bytes 9568256 | tf_op jit(solution)/shard_map/dot_general | solution.py:63
  129.9 0.0 reduce-scatter.5.cloned.1.call-update
  129.9 9.7 %reduce-scatter.3.cloned.1.call-done = bf16[64,1664]{1,0:T(8,128)(2,1)} async-done(((bf16[256,1664]{1,0:T(8,128)(2,1)}), bf16[64,1664]{1,0:T(8,128)(2,1)}) %reduce-scatter.3.cloned.1.call-update) | async-done | bytes 213008 | tf_op jit(solution)/shard_map/reduce_scatter | solution.py:52
  139.6 1.7 reshape.28
  141.3 48.9 %all_to_all.15 = bf16[32,2,1664]{2,1,0:T(2,128)(2,1)} all-to-all(bf16[32,2,1664]{2,1,0:T(2,128)(2,1)} %reshape.28), channel_id=1, replica_groups=mesh['expert'=32,'fsdp'=4,'dp'=8] {'expert'}, dimensions={0} | all-to-all | bytes 425984 | tf_op jit(solution)/shard_map/all_to_all | solution.py:54
  190.2 1.7 reshape.29
  191.9 2.3 convolution_convert_fusion.1
  194.2 280.3 %reduce-scatter.5.cloned.1.call-done = bf16[128,1664]{1,0:T(8,128)(2,1)} async-done(((bf16[1024,1664]{1,0:T(8,128)(2,1)}), bf16[128,1664]{1,0:T(8,128)(2,1)}) %reduce-scatter.5.cloned.1.call-update) | async-done | bytes 426000 | tf_op jit(solution)/shard_map/reduce_scatter | solution.py:66
  474.4 2.0 bitcast_convert_fusion
Async XLA Ops:
  7.2 91.9 %copy-start = (bf16[1,1024,1664]{2,1,0:T(8,128)(2,1)S(1)}, bf16[1,1024,1664]{2,1,0:T(8,128)(2,1)}, u32[]{:S(2)}) copy-start(bf16[1,1024,1664]{2,1,0:T(8,128)(2,1)} %param.11) | copy-start | bytes 10223620
  11.9 56.3 %all-to-all-start = ((bf16[32,2,1664]{2,1,0:T(2,128)(2,1)}), bf16[32,2,1664]{2,1,0:T(2,128)(2,1)}, u32[]{:S(2)}, u32[]{:S(2)}) async-start(bf16[32,2,1664]{2,1,0:T(2,128)(2,1)} %reshape.26), calls=%async_computation | async-start | bytes 425984 | tf_op jit(solution)/shard_map/all_to_all | solution.py:31
  68.1 39.6 %all-to-all-start.2 = ((bf16[32,2,1664]{2,1,0:T(2,128)(2,1)}), bf16[32,2,1664]{2,1,0:T(2,128)(2,1)}, u32[]{:S(2)}, u32[]{:S(2)}) async-start(bf16[32,2,1664]{2,1,0:T(2,128)(2,1)} %reshape.30), calls=%async_computation.3 | async-start | bytes 425984 | tf_op jit(solution)/shard_map/all_to_all | solution.py:32
  77.7 61.9 %reduce-scatter.3.cloned.1.call-start = ((), (), s32[]{:S(2)}) async-start(), calls=%async_computation.5 | async-start | bytes 1064960 | tf_op jit(solution)/shard_map/reduce_scatter | solution.py:52
  94.0 0.9 copy-start.1
  98.1 1.0 copy-start.2
  101.1 373.3 %reduce-scatter.5.cloned.1.call-start = ((), (), s32[]{:S(2)}) async-start(), calls=%async_computation.6 | async-start | bytes 3833856 | tf_op jit(solution)/shard_map/reduce_scatter | solution.py:66
Sparse Core Ops, SparseCore 0:
  101.2 38.3 reduce-scatter.2
  146.6 327.7 reduce-scatter.4
where the time goes:
time: 484 us; the launch traced here: 483 us
  waiting for transfers between devices  322 us (67%)
  blocking collectives  78.1 us (16%)
  starting transfers between devices  35.9 us (7%)
  matrix products  17.2 us (4%)
  between operations  14.1 us (3%)
  local copies, waits for them, and re-layouts  13.9 us (3%)
    reduce_scatter x1, waiting for transfers between devices, body(): lax.psum_scatter(term.astype(jnp.bfloat16), 'dp', scatter_dimension=0, ti...  280 us
    all_to_all x1, blocking collectives, body(): lax.all_to_all(expert_out, 'expert', split_axis=0, concat_axis=0, tiled=T...  48.9 us
    all_to_all x1, starting transfers between devices, body(): lax.all_to_all(slot_in, 'expert', split_axis=0, concat_axis=0, tiled=True)  26.3 us
    all_to_all x1, waiting for transfers between devices, body(): lax.all_to_all(slot_in, 'expert', split_axis=0, concat_axis=0, tiled=True)  25.5 us
    all_gather x1, blocking collectives, body(): g_rows = lax.all_gather(g_mine, 'fsdp', axis=0, tiled=True)  14.7 us
    all_gather x1, blocking collectives, body(): x_rows = lax.all_gather(x_mine, 'fsdp', axis=0, tiled=True)  14.6 us
    reduce_scatter x1, waiting for transfers between devices, body(): lax.psum_scatter(out_buf.astype(jnp.bfloat16), 'fsdp', scatter_dimension=...  9.69 us
  transfers between devices with their start and end apart: 4, of which 4 were waited for; matrix products, arithmetic and copies ran while one was open for 5% of the time, Pallas kernels for 0%

commit v1 on v0

v1 whole, which is shorter than its diff:
```python
import functools

import jax
import jax.numpy as jnp
from jax import lax
from jax.experimental import pallas as pl
from jax.experimental.pallas import tpu as pltpu
from jax.sharding import PartitionSpec as P

MESH = pl.DeviceIdType.MESH
BF16 = jnp.bfloat16
F32 = jnp.float32
NT = (((1,), (1,)), ((), ()))


def gelu_parts(value):
    normal_cdf = 0.5 * (1.0 + lax.erf(value * 0.7071067811865476))
    normal_pdf = jnp.exp(-0.5 * value * value) * 0.3989422804014327
    return (value * normal_cdf, normal_cdf + value * normal_pdf)


def column_pieces(width):
    unit = 128
    total = width // unit
    if total < 5:
        return [(i * unit, unit) for i in range(total)]
    sizes = [2]
    rest = total - 2
    parts = 3
    for i in range(parts):
        sizes.append(rest // parts + (1 if i < rest % parts else 0))
    pieces, start = [], 0
    for size in sizes:
        pieces.append((start * unit, size * unit))
        start += size
    return pieces


def layer_kernel(
    dims, idx_col, gate_col, idx_row, gate_row, tokens, grad_out, w_in, w_out,
    mixed, weight_grad,
    win, wout, snd, xg, xs, gs, act, slope, dpre_t, po, po_in, own_po, back_rows, ret,
    gsend, gin, gown, zsend, zin,
    w_sem, z_send, z_recv, x_send, x_recv, po_send, po_recv, r_send, r_recv,
    y_send, y_recv, zz_send, zz_recv,
):
    zl_n, x_n, y_n = dims
    z_n = 2 * zl_n
    half = zl_n // 2
    rounds = zl_n - 1
    experts = 2 * zl_n
    width = tokens.shape[1]
    toks = tokens.shape[0]
    hid = w_in.shape[0]
    slots = 2 * experts
    rows = x_n * slots
    block = hid // (2 * y_n)
    e_me = lax.axis_index("expert")
    x_me = lax.axis_index("fsdp")
    d_me = lax.axis_index("dp")
    core = e_me % 2
    zh = d_me // y_n
    y_me = d_me % y_n
    z_me = zh * zl_n + e_me // 2

    def at_z(z, c):
        return ((z % zl_n) * 2 + c, x_me, (z // zl_n) * y_n + y_me)

    def at_x(step):
        return (e_me, (x_me + step) % x_n, d_me)

    def at_y(step):
        return (e_me, x_me, zh * y_n + (y_me + step) % y_n)

    def distance(t, c):
        return (t // 2 + 1) * (1 - 2 * (t % 2)) - z_n // 2 * c * (t // (rounds - 1))

    mate = at_z(z_me, 1 - core)
    across = at_z((z_me + zl_n) % z_n, core)

    win_copy = pltpu.make_async_copy(w_in, win, w_sem.at[0])
    wout_copy = pltpu.make_async_copy(w_out, wout, w_sem.at[1])
    win_copy.start()
    wout_copy.start()

    barrier = pltpu.get_barrier_semaphore()

    def greet(device):
        pl.semaphore_signal(barrier, inc=1, device_id=device, device_id_type=MESH)

    def greet_z(i, carry):
        t = i // 2
        c = i % 2
        dz = (t // 2 + 1) * (1 - 2 * (t % 2))
        greet(at_z((z_me + dz + z_n) % z_n, c))
        return carry

    lax.fori_loop(0, 2 * (rounds - 1), greet_z, 0)
    greet(at_z((z_me + half) % z_n, 0))
    greet(at_z((z_me - half + z_n) % z_n, 1))
    greet(at_z((z_me - half + zl_n * core + z_n) % z_n, core))
    greet(mate)
    greet(across)
    for j in range(1, x_n):
        greet(at_x(j))
    for j in range(1, y_n):
        greet(at_y(j))

    lane = lax.broadcasted_iota(jnp.int32, (2 * slots, 2 * toks), 1)
    pick = (idx_col[...] == lane).astype(F32).astype(BF16)
    both = jnp.concatenate([tokens[...], grad_out[...]], axis=0)
    picked = jnp.dot(pick, both, preferred_element_type=F32) * gate_col[...]
    snd[...] = picked.astype(BF16).reshape(experts, 4, width)

    pl.semaphore_wait(barrier, 2 * (rounds - 1) + 3 + 2 + (x_n - 1) + (y_n - 1))

    def z_copy(i):
        t = i // 2
        c = i % 2
        z_to = (z_me + distance(t, c) + z_n) % z_n
        return pltpu.make_async_remote_copy(
            src_ref=snd.at[(z_to % zl_n) * 2 + c],
            dst_ref=xg.at[0, 2 + 2 * t + core],
            send_sem=z_send.at[2 + i],
            recv_sem=z_recv.at[2 + 2 * t + core],
            device_id=at_z(z_to, c),
            device_id_type=MESH,
        )

    def z_start(i, carry):
        z_copy(i).start()
        return carry

    lax.fori_loop(0, 2 * rounds, z_start, 0)
    mate_copy = pltpu.make_async_remote_copy(
        src_ref=snd.at[e_me + 1 - 2 * core],
        dst_ref=xg.at[0, core],
        send_sem=z_send.at[0],
        recv_sem=z_recv.at[core],
        device_id=mate,
        device_id_type=MESH,
    )
    mate_copy.start()
    xg[0, pl.ds(core, 1)] = snd[pl.ds(e_me, 1)]

    def z_arrived(k):
        pltpu.make_async_remote_copy(
            src_ref=snd.at[0], dst_ref=xg.at[0, k], send_sem=z_send.at[0],
            recv_sem=z_recv.at[k], device_id=mate, device_id_type=MESH,
        ).wait_recv()

    groups = 4
    per = experts // groups

    def x_copy(g, j):
        return pltpu.make_async_remote_copy(
            src_ref=xg.at[0, pl.ds(per * g, per)],
            dst_ref=xg.at[j, pl.ds(per * g, per)],
            send_sem=x_send.at[g, j],
            recv_sem=x_recv.at[g, j],
            device_id=at_x(j),
            device_id_type=MESH,
        )

    for g in range(groups):
        first = 2 if g == 0 else per * g
        if g == 0:
            z_arrived(1 - core)

        def wait_one(k, carry):
            z_arrived(k)
            return carry

        lax.fori_loop(first, per * (g + 1), wait_one, 0)
        for j in range(1, x_n):
            x_copy(g, j).start()
    for g in range(groups):
        for j in range(1, x_n):
            x_copy(g, j).wait_recv()

    everything = xg[...].reshape(x_n * experts, 4, width)
    xs[...] = everything[:, 0:2].reshape(rows, width)
    gs[...] = everything[:, 2:4].reshape(rows, width)

    win_copy.wait()
    wout_copy.wait()
    hb = min(256, hid)

    def project(b, carry):
        at = pl.ds(pl.multiple_of(b * hb, hb), hb)
        pre = lax.dot_general(xs[...], win[at], NT, preferred_element_type=F32)
        value, tilt = gelu_parts(pre)
        act[:, at] = value.astype(BF16)
        slope[:, at] = tilt
        return carry

    lax.fori_loop(0, hid // hb, project, 0)
    for start in range(0, width, 256):
        cols = slice(start, min(start + 256, width))
        part = jnp.dot(act[...], wout[:, cols], preferred_element_type=F32)
        own_po[:, cols] = part[0:slots]
        po[:, :, :, cols] = part[slots:rows].astype(BF16).reshape(x_n - 1, experts, 2, cols.stop - cols.start)

    def po_copy(j):
        return pltpu.make_async_remote_copy(
            src_ref=po.at[j - 1],
            dst_ref=po_in.at[j - 1],
            send_sem=po_send.at[j - 1],
            recv_sem=po_recv.at[j - 1],
            device_id=at_x(x_n - j),
            device_id_type=MESH,
        )

    for j in range(1, x_n):
        po_copy(j).start()

    def cotangent(b, carry):
        at = pl.ds(pl.multiple_of(b * hb, hb), hb)
        back = lax.dot_general(gs[...], wout[at], NT, preferred_element_type=F32)
        dpre_t[at] = (back * slope[:, at]).T.astype(BF16)
        return carry

    lax.fori_loop(0, hid // hb, cotangent, 0)

    pieces = column_pieces(width)
    quarter = y_n * block

    def y_copy(side, p, j):
        cols = pl.ds(*pieces[p])
        return pltpu.make_async_remote_copy(
            src_ref=gsend.at[side, (y_me + j) % y_n, :, cols],
            dst_ref=gin.at[side, j - 1, :, cols],
            send_sem=y_send.at[side, p, j - 1],
            recv_sem=y_recv.at[side, p, j - 1],
            device_id=at_y(j),
            device_id_type=MESH,
        )

    def gradients(side):
        where = (zh + 1 - side) % 2
        mine = dpre_t[pl.ds(pl.multiple_of(where * quarter, quarter), quarter)]
        for p, (start, size) in enumerate(pieces):
            for at in range(start, start + size, 256):
                cols = slice(at, min(at + 256, start + size))
                term = jnp.dot(mine, xs[:, cols], preferred_element_type=F32)
                gsend[side, :, :, cols] = term.astype(BF16).reshape(y_n, block, cols.stop - cols.start)
            for j in range(1, y_n):
                y_copy(side, p, j).start()

    def summed(side, p):
        start, size = pieces[p]
        cols = slice(start, start + size)
        for j in range(1, y_n):
            y_copy(side, p, j).wait_recv()
        total = gsend[side, pl.ds(y_me, 1), :, cols][0].astype(F32)
        for j in range(1, y_n):
            total = total + gin[side, j - 1, :, cols].astype(F32)
        return total

    def zz_copy(p):
        cols = pl.ds(*pieces[p])
        return pltpu.make_async_remote_copy(
            src_ref=zsend.at[:, cols],
            dst_ref=zin.at[:, cols],
            send_sem=zz_send.at[p],
            recv_sem=zz_recv.at[p],
            device_id=across,
            device_id_type=MESH,
        )

    def cross(p):
        start, size = pieces[p]
        zsend[:, start:start + size] = summed(0, p).astype(BF16)
        zz_copy(p).start()

    gradients(0)
    cross(0)

    for j in range(1, x_n):
        po_copy(j).wait_recv()
    out = own_po[...]
    for j in range(1, x_n):
        out = out + po_in[j - 1].reshape(slots, width).astype(F32)
    back_rows[...] = out.astype(BF16).reshape(experts, 2, width)

    def ret_copy(i):
        t = i // 2
        c = i % 2
        z_to = (z_me - distance(t, core) + z_n) % z_n
        return pltpu.make_async_remote_copy(
            src_ref=back_rows.at[2 + i],
            dst_ref=ret.at[e_me],
            send_sem=r_send.at[2 + i],
            recv_sem=r_recv.at[e_me],
            device_id=at_z(z_to, c),
            device_id_type=MESH,
        )

    def ret_start(i, carry):
        ret_copy(i).start()
        return carry

    lax.fori_loop(0, 2 * rounds, ret_start, 0)
    mate_back = pltpu.make_async_remote_copy(
        src_ref=back_rows.at[1 - core],
        dst_ref=ret.at[e_me],
        send_sem=r_send.at[0],
        recv_sem=r_recv.at[e_me],
        device_id=mate,
        device_id_type=MESH,
    )
    mate_back.start()
    ret[pl.ds(e_me, 1)] = back_rows[pl.ds(core, 1)]

    for p in range(1, len(pieces)):
        cross(p)
    gradients(1)

    def ret_arrived(e):
        pltpu.make_async_remote_copy(
            src_ref=back_rows.at[0], dst_ref=ret.at[e], send_sem=r_send.at[0],
            recv_sem=r_recv.at[e], device_id=mate, device_id_type=MESH,
        ).wait_recv()

    def ret_wait(i, carry):
        c = i % 2
        z_from = (z_me + distance(i // 2, c) + z_n) % z_n
        ret_arrived((z_from % zl_n) * 2 + c)
        return carry

    lax.fori_loop(0, 2 * rounds, ret_wait, 0)
    ret_arrived(e_me + 1 - 2 * core)
    token = lax.broadcasted_iota(jnp.int32, (toks, slots), 0)
    weight = jnp.where(token == idx_row[...], gate_row[...], 0.0)
    high = weight.astype(BF16)
    rest = weight - high.astype(F32)
    middle = rest.astype(BF16)
    low = (rest - middle.astype(F32)).astype(BF16)
    came = ret[...].reshape(slots, width)
    total = jnp.dot(low, came, preferred_element_type=F32)
    total = total + jnp.dot(middle, came, preferred_element_type=F32)
    total = total + jnp.dot(high, came, preferred_element_type=F32)
    mixed[...] = total.astype(BF16)

    for p, (start, size) in enumerate(pieces):
        near = summed(1, p)
        zz_copy(p).wait_recv()
        cols = slice(start, start + size)
        weight_grad[:, cols] = near + zin[:, cols].astype(F32)

    def z_sent(i, carry):
        z_copy(i).wait_send()
        ret_copy(i).wait_send()
        return carry

    lax.fori_loop(0, 2 * rounds, z_sent, 0)
    mate_copy.wait_send()
    mate_back.wait_send()
    for g in range(groups):
        for j in range(1, x_n):
            x_copy(g, j).wait_send()
    for j in range(1, x_n):
        po_copy(j).wait_send()
    for p in range(len(pieces)):
        for side in range(2):
            for j in range(1, y_n):
                y_copy(side, p, j).wait_send()
        zz_copy(p).wait_send()


def body(zl_n, y_n, x_n, tokens, grad_out, slot_token, slot_gate, w_in, w_out):
    experts = 2 * zl_n
    toks, width = tokens.shape
    hid = w_in.shape[1]
    slots = 2 * experts
    rows = x_n * slots
    block = hid // (2 * y_n)
    place = slot_token.reshape(experts, 2)
    gate = slot_gate.reshape(experts, 2)
    idx_col = jnp.concatenate([place, place + toks], axis=1).reshape(2 * slots, 1)
    gate_col = jnp.concatenate([jnp.ones_like(gate), gate], axis=1).reshape(2 * slots, 1)
    pieces = len(column_pieces(width))
    vmem = pl.BlockSpec(memory_space=pltpu.VMEM)
    hbm = pl.BlockSpec(memory_space=pl.ANY)
    dma = pltpu.SemaphoreType.DMA
    mixed, weight_grad = pl.pallas_call(
        functools.partial(layer_kernel, (zl_n, x_n, y_n)),
        out_shape=(
            jax.ShapeDtypeStruct((toks, width), BF16),
            jax.ShapeDtypeStruct((block, width), F32),
        ),
        in_specs=[vmem] * 6 + [hbm] * 2,
        out_specs=(vmem, vmem),
        scratch_shapes=[
            pltpu.VMEM((hid, width), BF16),
            pltpu.VMEM((hid, width), BF16),
            pltpu.VMEM((experts, 4, width), BF16),
            pltpu.VMEM((x_n, experts, 4, width), BF16),
            pltpu.VMEM((rows, width), BF16),
            pltpu.VMEM((rows, width), BF16),
            pltpu.VMEM((rows, hid), BF16),
            pltpu.VMEM((rows, hid), F32),
            pltpu.VMEM((hid, rows), BF16),
            pltpu.VMEM((x_n - 1, experts, 2, width), BF16),
            pltpu.VMEM((x_n - 1, experts, 2, width), BF16),
            pltpu.VMEM((slots, width), F32),
            pltpu.VMEM((experts, 2, width), BF16),
            pltpu.VMEM((experts, 2, width), BF16),
            pltpu.VMEM((2, y_n, block, width), BF16),
            pltpu.VMEM((2, y_n - 1, block, width), BF16),
            pltpu.VMEM((8, 128), F32),
            pltpu.VMEM((block, width), BF16),
            pltpu.VMEM((block, width), BF16),
            dma((2,)),
            dma((experts,)),
            dma((experts,)),
            dma((4, x_n)),
            dma((4, x_n)),
            dma((x_n,)),
            dma((x_n,)),
            dma((experts,)),
            dma((experts,)),
            dma((2, pieces, y_n)),
            dma((2, pieces, y_n)),
            dma((pieces,)),
            dma((pieces,)),
        ],
        compiler_params=pltpu.CompilerParams(
            collective_id=0, has_side_effects=True, vmem_limit_bytes=56 * 1024 * 1024
        ),
    )(
        idx_col, gate_col, slot_token.reshape(1, slots), slot_gate.reshape(1, slots),
        tokens, grad_out, w_in[0], w_out[0],
    )
    return mixed, weight_grad[None]


def solution(mesh):
    placed = (
        P(("expert", "fsdp", "dp"), None),
        P(("expert", "fsdp", "dp"), None),
        P(("expert", "fsdp", "dp"), None, None),
        P(("expert", "fsdp", "dp"), None, None),
        P("expert", "fsdp", None),
        P("expert", "fsdp", None),
    )
    sizes = (mesh.shape["expert"] // 2, mesh.shape["dp"] // 2, mesh.shape["fsdp"])
    return jax.shard_map(
        functools.partial(body, *sizes),
        mesh=mesh,
        in_specs=placed,
        out_specs=(P(("expert", "fsdp", "dp"), None), P("expert", ("fsdp", "dp"), None)),
        check_vma=False,
    )
```

time: 484 us -> 175 us (0.36)
  the two profiles are of different devices: /device:TPU:6 before, /device:TPU:129 now
where the time goes in v1:
time: 175 us
  Pallas kernels  164 us (94%)
  local copies, waits for them, and re-layouts  9.12 us (5%)
    pallas_call x1, Pallas kernels, body(): pl.pallas_call(functools.partial(layer_kernel, (zl_n, x_n, y_n)), out_sha...  164 us
    unnamed x5, local copies, waits for them, and re-layouts  6.18 us

profile of v1, /device:TPU:129, one launch (start us, length us, event | category | flops | bytes accessed | tf_op | source)
XLA Modules:
  0.0 175.0 jit_solution(3254537260562875124)
XLA Ops:
  0.6 0.7 broadcast_add_fusion
  1.3 0.7 pad_add_fusion
  2.0 0.1 copy.14
  2.1 0.8 copy.20
  2.8 0.1 concatenate.7.clone
  2.9 0.8 copy.17
  3.7 0.7 reshape.27.gate_row
  4.3 0.8 copy.16
  5.1 0.7 reshape.26.idx_row
  5.8 0.7 reshape.29.gate_col
  6.5 0.7 reshape.28.idx_col
  7.2 163.9 %shard_map.77 = (bf16[128,1664]{1,0:T(8,128)(2,1)}, f32[128,1664]{1,0:T(8,128)}) custom-call(s32[128,1]{1,0:T(8,128)} %reshape.28.idx_col, f32[128,1]{1,0:T(8,128)} %reshape.29.gate_col, s32[1,64]{1,0:T(1,128)} %reshape.26.idx_row, f32[1,64]{1,0:T(1,128)} %reshape.27.gate_row, bf16[128,1664]{1,0:T(8,128)(2,1)} %tokens.1, bf16[128,1664]{1,0:T(8,128)(2,1)} %grad_out.1, ...), custom_call_target="tpu_custom_call" | custom-call | tf_op jit(solution)/shard_map/pallas_call | solution.py:386
  171.1 1.8 %copy.23 = bf16[128,1664]{1,0:T(8,128)(2,1)} copy(bf16[128,1664]{1,0:T(8,128)(2,1)} %get-tuple-element.8) | data formatting | bytes 851968
  172.9 2.1 %copy.24 = f32[1,128,1664]{2,1,0:T(8,128)} copy(f32[1,128,1664]{2,1,0:T(8,128)} %bitcast.8) | data formatting | bytes 1703936

commit v2 on v1

v2 whole, which is shorter than its diff:
```python
import functools

import jax
import jax.numpy as jnp
from jax import lax
from jax.experimental import pallas as pl
from jax.experimental.pallas import tpu as pltpu
from jax.sharding import PartitionSpec as P

MESH = pl.DeviceIdType.MESH
BF16 = jnp.bfloat16
F32 = jnp.float32
NT = (((1,), (1,)), ((), ()))


def gelu_parts(value):
    normal_cdf = 0.5 * (1.0 + lax.erf(value * 0.7071067811865476))
    normal_pdf = jnp.exp(-0.5 * value * value) * 0.3989422804014327
    return (value * normal_cdf, normal_cdf + value * normal_pdf)


def column_pieces(width):
    unit = 128
    units = width // unit
    sizes, left = [], units
    for size in (1, 2, 3, 3):
        if left > size:
            sizes.append(size)
            left -= size
    sizes.append(left)
    pieces, start = [], 0
    for size in sizes:
        pieces.append((start * unit, size * unit))
        start += size
    return pieces


def arrival_groups(experts):
    edges = [0]
    for tail in (22, 14, 6, 2, 0):
        if experts - tail > edges[-1]:
            edges.append(experts - tail)
    return list(zip(edges[:-1], edges[1:]))


def layer_kernel(
    dims, place, gate, tokens, grad_out, w_in, w_out,
    mixed, weight_grad,
    win, wout, snd, xg, xs, gs, act, dpre_t, po, po_in, own_po, back_rows, ret,
    gsend, gin, zsend, zin,
    w_sem, z_send, z_recv, x_send, x_recv, po_send, po_recv, r_send, r_recv,
    y_send, y_recv, zz_send, zz_recv,
):
    zl_n, x_n, y_n = dims
    z_n = 2 * zl_n
    half = zl_n // 2
    experts = 2 * zl_n
    width = tokens.shape[1]
    toks = tokens.shape[0]
    hid = w_in.shape[0]
    slots = 2 * experts
    rows = x_n * slots
    block = hid // (2 * y_n)
    e_me = lax.axis_index("expert")
    x_me = lax.axis_index("fsdp")
    d_me = lax.axis_index("dp")
    core = lax.rem(e_me, 2)
    zh = lax.div(d_me, y_n)
    y_me = lax.rem(d_me, y_n)
    z_me = zh * zl_n + lax.div(e_me, 2)

    def wrap(z):
        return lax.rem(z + z_n, z_n)

    def expert_at(z, c):
        return lax.rem(z, zl_n) * 2 + c

    def at_z(z, c):
        return (expert_at(z, c), x_me, lax.div(z, zl_n) * y_n + y_me)

    def at_x(step):
        return (e_me, lax.rem(x_me + step, x_n), d_me)

    def at_y(step):
        return (e_me, x_me, zh * y_n + lax.rem(y_me + step, y_n))

    mate = at_z(z_me, 1 - core)
    across = at_z(wrap(z_me + zl_n), core)

    win_copy = pltpu.make_async_copy(w_in, win, w_sem.at[0])
    wout_copy = pltpu.make_async_copy(w_out, wout, w_sem.at[1])
    win_copy.start()
    wout_copy.start()

    barrier = pltpu.get_barrier_semaphore()

    def greet(device):
        pl.semaphore_signal(barrier, inc=1, device_id=device, device_id_type=MESH)

    def greet_z(m, carry):
        for z in (wrap(z_me + m), wrap(z_me - m)):
            for c in (0, 1):
                greet(at_z(z, c))
        return carry

    lax.fori_loop(1, half, greet_z, 0)
    greet(at_z(wrap(z_me + half), 0))
    greet(at_z(wrap(z_me - half), 1))
    greet(at_z(wrap(z_me - half + zl_n * core), core))
    greet(mate)
    greet(across)
    for j in range(1, x_n):
        greet(at_x(j))
    for j in range(1, y_n):
        greet(at_y(j))

    def column(table, rows, per):
        row = lax.broadcasted_iota(jnp.int32, (rows, experts), 0)
        lane = lax.broadcasted_iota(jnp.int32, (rows, experts), 1)
        value = jnp.where((row & 1) == 0, table[0:1].astype(F32), table[1:2].astype(F32))
        mine = lax.shift_right_logical(row, per) == lane
        return jnp.sum(jnp.where(mine, value, 0.0), axis=1, keepdims=True)

    row = lax.broadcasted_iota(jnp.int32, (2 * slots, 1), 0)
    is_grad = (row & 2) == 2
    wanted = column(place[...], 2 * slots, 2) + jnp.where(is_grad, float(toks), 0.0)
    scale = jnp.where(is_grad, column(gate[...], 2 * slots, 2), 1.0)
    lane = lax.broadcasted_iota(jnp.int32, (2 * slots, 2 * toks), 1).astype(F32)
    pick = (wanted == lane).astype(F32).astype(BF16)
    both = jnp.concatenate([tokens[...], grad_out[...]], axis=0)
    picked = jnp.dot(pick, both, preferred_element_type=F32) * scale
    snd[...] = picked.astype(BF16).reshape(experts, 4, width)

    pl.semaphore_wait(barrier, 4 * (half - 1) + 3 + 2 + (x_n - 1) + (y_n - 1))

    def z_copy(z_to, c, slot):
        return pltpu.make_async_remote_copy(
            src_ref=snd.at[expert_at(z_to, c)],
            dst_ref=xg.at[0, slot + core],
            send_sem=z_send.at[slot + c],
            recv_sem=z_recv.at[slot + core],
            device_id=at_z(z_to, c),
            device_id_type=MESH,
        )

    mate_copy = pltpu.make_async_remote_copy(
        src_ref=snd.at[e_me + 1 - 2 * core],
        dst_ref=xg.at[0, core],
        send_sem=z_send.at[0],
        recv_sem=z_recv.at[core],
        device_id=mate,
        device_id_type=MESH,
    )
    mate_copy.start()
    xg[0, pl.ds(core, 1)] = snd[pl.ds(e_me, 1)]

    for c in (0, 1):

        def z_start(m, carry):
            slot = 4 * m - 2
            z_copy(wrap(z_me + m), c, slot).start()
            z_copy(wrap(z_me - m), c, slot + 2).start()
            return carry

        lax.fori_loop(1, half, z_start, 0)
        z_copy(wrap(z_me + half - zl_n * c), c, experts - 2).start()
    def z_arrived(k):
        pltpu.make_async_remote_copy(
            src_ref=snd.at[0], dst_ref=xg.at[0, k], send_sem=z_send.at[0],
            recv_sem=z_recv.at[k], device_id=mate, device_id_type=MESH,
        ).wait_recv()

    groups = arrival_groups(experts)

    def x_copy(g, j):
        first, last = groups[g]
        return pltpu.make_async_remote_copy(
            src_ref=xg.at[0, pl.ds(first, last - first)],
            dst_ref=xg.at[j, pl.ds(first, last - first)],
            send_sem=x_send.at[g, j],
            recv_sem=x_recv.at[g, j],
            device_id=at_x(j),
            device_id_type=MESH,
        )

    def wait_one(k, carry):
        z_arrived(k)
        return carry

    z_arrived(1 - core)
    for g, (first, last) in enumerate(groups):
        lax.fori_loop(max(first, 2), last, wait_one, 0)
        for j in range(1, x_n):
            x_copy(g, j).start()
    for g in range(len(groups)):
        for j in range(1, x_n):
            x_copy(g, j).wait_recv()

    everything = xg[...].reshape(x_n * experts, 4, width)
    xs[...] = everything[:, 0:2].reshape(rows, width)
    gs[...] = everything[:, 2:4].reshape(rows, width)

    win_copy.wait()
    wout_copy.wait()
    quarter = y_n * block
    hb = min(256, quarter)

    def hidden(side):
        def one(b, carry):
            at = pl.ds(pl.multiple_of(lax.rem(zh + 1 - side, 2) * quarter + b * hb, hb), hb)
            pre = lax.dot_general(xs[...], win[at], NT, preferred_element_type=F32)
            value, slope = gelu_parts(pre)
            act[:, at] = value.astype(BF16)
            back = lax.dot_general(gs[...], wout[at], NT, preferred_element_type=F32)
            dpre_t[at] = (back * slope).T.astype(BF16)
            return carry

        lax.fori_loop(0, quarter // hb, one, 0)

    def project_out():
        for start in range(0, width, 256):
            cols = slice(start, min(start + 256, width))
            part = jnp.dot(act[...], wout[:, cols], preferred_element_type=F32)
            own_po[:, cols] = part[0:slots]
            po[:, :, :, cols] = part[slots:rows].astype(BF16).reshape(x_n - 1, experts, 2, cols.stop - cols.start)
        for j in range(1, x_n):
            po_copy(j).start()

    def po_copy(j):
        return pltpu.make_async_remote_copy(
            src_ref=po.at[j - 1],
            dst_ref=po_in.at[j - 1],
            send_sem=po_send.at[j - 1],
            recv_sem=po_recv.at[j - 1],
            device_id=at_x(x_n - j),
            device_id_type=MESH,
        )

    pieces = column_pieces(width)

    def y_copy(side, p, j):
        cols = pl.ds(*pieces[p])
        return pltpu.make_async_remote_copy(
            src_ref=gsend.at[side, lax.rem(y_me + j, y_n), :, cols],
            dst_ref=gin.at[side, j - 1, :, cols],
            send_sem=y_send.at[side, p, j - 1],
            recv_sem=y_recv.at[side, p, j - 1],
            device_id=at_y(j),
            device_id_type=MESH,
        )

    def gradient(side, p):
        where = lax.rem(zh + 1 - side, 2)
        mine = dpre_t[pl.ds(pl.multiple_of(where * quarter, quarter), quarter)]
        start, size = pieces[p]
        for at in range(start, start + size, 256):
            cols = slice(at, min(at + 256, start + size))
            term = jnp.dot(mine, xs[:, cols], preferred_element_type=F32)
            gsend[side, :, :, cols] = term.astype(BF16).reshape(y_n, block, cols.stop - cols.start)
        for j in range(1, y_n):
            y_copy(side, p, j).start()

    def summed(side, p):
        start, size = pieces[p]
        cols = slice(start, start + size)
        for j in range(1, y_n):
            y_copy(side, p, j).wait_recv()
        total = gsend[side, pl.ds(y_me, 1), :, cols][0].astype(F32)
        for j in range(1, y_n):
            total = total + gin[side, j - 1, :, cols].astype(F32)
        return total

    def zz_copy(p):
        cols = pl.ds(*pieces[p])
        return pltpu.make_async_remote_copy(
            src_ref=zsend.at[:, cols],
            dst_ref=zin.at[:, cols],
            send_sem=zz_send.at[p],
            recv_sem=zz_recv.at[p],
            device_id=across,
            device_id_type=MESH,
        )

    def cross(p):
        start, size = pieces[p]
        zsend[:, start:start + size] = summed(0, p).astype(BF16)
        zz_copy(p).start()

    hidden(0)
    for p in range(min(2, len(pieces))):
        gradient(0, p)
    hidden(1)
    cross(0)
    for p in range(2, len(pieces)):
        gradient(0, p)
    cross(1)
    project_out()
    for p in range(2, len(pieces)):
        cross(p)

    for j in range(1, x_n):
        po_copy(j).wait_recv()
    out = own_po[...]
    for j in range(1, x_n):
        out = out + po_in[j - 1].reshape(slots, width).astype(F32)
    back_rows[...] = out.astype(BF16).reshape(experts, 2, width)

    def ret_copy(z_to, c, slot):
        return pltpu.make_async_remote_copy(
            src_ref=back_rows.at[slot + c],
            dst_ref=ret.at[e_me],
            send_sem=r_send.at[slot + c],
            recv_sem=r_recv.at[e_me],
            device_id=at_z(z_to, c),
            device_id_type=MESH,
        )

    def ret_start(m, carry):
        slot = 4 * m - 2
        for z, add in ((wrap(z_me - m), 0), (wrap(z_me + m), 2)):
            for c in (0, 1):
                ret_copy(z, c, slot + add).start()
        return carry

    lax.fori_loop(1, half, ret_start, 0)
    for c in (0, 1):
        ret_copy(wrap(z_me - half + zl_n * core), c, experts - 2).start()
    mate_back = pltpu.make_async_remote_copy(
        src_ref=back_rows.at[1 - core],
        dst_ref=ret.at[e_me],
        send_sem=r_send.at[0],
        recv_sem=r_recv.at[e_me],
        device_id=mate,
        device_id_type=MESH,
    )
    mate_back.start()
    ret[pl.ds(e_me, 1)] = back_rows[pl.ds(core, 1)]

    for p in range(len(pieces)):
        gradient(1, p)

    def z_sent(k, carry):
        pltpu.make_async_remote_copy(
            src_ref=snd.at[0], dst_ref=xg.at[0, 0], send_sem=z_send.at[k],
            recv_sem=z_recv.at[0], device_id=mate, device_id_type=MESH,
        ).wait_send()
        return carry

    lax.fori_loop(2, experts, z_sent, 0)
    mate_copy.wait_send()
    for g in range(len(groups)):
        for j in range(1, x_n):
            x_copy(g, j).wait_send()
    for j in range(1, x_n):
        po_copy(j).wait_send()

    for p, (start, size) in enumerate(pieces):
        weight_grad[:, start:start + size] = summed(1, p)
    token = lax.broadcasted_iota(jnp.int32, (slots, toks), 1).astype(F32)
    chosen = column(place[...], slots, 1) == token
    weight = jnp.where(chosen, column(gate[...], slots, 1), 0.0).T
    high = weight.astype(BF16)
    rest = weight - high.astype(F32)
    middle = rest.astype(BF16)
    low = (rest - middle.astype(F32)).astype(BF16)
    weights = jnp.concatenate([low, middle, high], axis=1)

    def ret_arrived(e, carry):
        pltpu.make_async_remote_copy(
            src_ref=back_rows.at[0], dst_ref=ret.at[e], send_sem=r_send.at[0],
            recv_sem=r_recv.at[e], device_id=mate, device_id_type=MESH,
        ).wait_recv()
        return carry

    lax.fori_loop(0, e_me, ret_arrived, 0)
    lax.fori_loop(e_me + 1, experts, ret_arrived, 0)
    came = ret[...].reshape(slots, width)
    came = jnp.concatenate([came, came, came], axis=0)
    mixed[...] = jnp.dot(weights, came, preferred_element_type=F32).astype(BF16)

    def ret_sent(k, carry):
        pltpu.make_async_remote_copy(
            src_ref=back_rows.at[0], dst_ref=ret.at[0], send_sem=r_send.at[k],
            recv_sem=r_recv.at[0], device_id=mate, device_id_type=MESH,
        ).wait_send()
        return carry

    lax.fori_loop(2, experts, ret_sent, 0)
    mate_back.wait_send()
    for p in range(len(pieces)):
        for side in range(2):
            for j in range(1, y_n):
                y_copy(side, p, j).wait_send()

    for p, (start, size) in enumerate(pieces):
        zz_copy(p).wait_recv()
        cols = slice(start, start + size)
        weight_grad[:, cols] += zin[:, cols].astype(F32)
    for p in range(len(pieces)):
        zz_copy(p).wait_send()


def body(zl_n, y_n, x_n, tokens, grad_out, slot_token, slot_gate, w_in, w_out):
    experts = 2 * zl_n
    toks, width = tokens.shape
    hid = w_in.shape[1]
    slots = 2 * experts
    rows = x_n * slots
    block = hid // (2 * y_n)
    groups = len(arrival_groups(experts))
    pieces = len(column_pieces(width))
    vmem = pl.BlockSpec(memory_space=pltpu.VMEM)
    hbm = pl.BlockSpec(memory_space=pl.ANY)
    dma = pltpu.SemaphoreType.DMA
    mixed, weight_grad = pl.pallas_call(
        functools.partial(layer_kernel, (zl_n, x_n, y_n)),
        out_shape=(
            jax.ShapeDtypeStruct((toks, width), BF16),
            jax.ShapeDtypeStruct((block, width), F32),
        ),
        in_specs=[vmem] * 4 + [hbm] * 2,
        out_specs=(vmem, vmem),
        scratch_shapes=[
            pltpu.VMEM((hid, width), BF16),
            pltpu.VMEM((hid, width), BF16),
            pltpu.VMEM((experts, 4, width), BF16),
            pltpu.VMEM((x_n, experts, 4, width), BF16),
            pltpu.VMEM((rows, width), BF16),
            pltpu.VMEM((rows, width), BF16),
            pltpu.VMEM((rows, hid), BF16),
            pltpu.VMEM((hid, rows), BF16),
            pltpu.VMEM((x_n - 1, experts, 2, width), BF16),
            pltpu.VMEM((x_n - 1, experts, 2, width), BF16),
            pltpu.VMEM((slots, width), F32),
            pltpu.VMEM((experts, 2, width), BF16),
            pltpu.VMEM((experts, 2, width), BF16),
            pltpu.VMEM((2, y_n, block, width), BF16),
            pltpu.VMEM((2, y_n - 1, block, width), BF16),
            pltpu.VMEM((block, width), BF16),
            pltpu.VMEM((block, width), BF16),
            dma((2,)),
            dma((experts,)),
            dma((experts,)),
            dma((groups, x_n)),
            dma((groups, x_n)),
            dma((x_n,)),
            dma((x_n,)),
            dma((experts,)),
            dma((experts,)),
            dma((2, pieces, y_n)),
            dma((2, pieces, y_n)),
            dma((pieces,)),
            dma((pieces,)),
        ],
        compiler_params=pltpu.CompilerParams(
            collective_id=0, has_side_effects=True, vmem_limit_bytes=56 * 1024 * 1024
        ),
    )(
        slot_token.reshape(experts, 2).T, slot_gate.reshape(experts, 2).T,
        tokens, grad_out, w_in[0], w_out[0],
    )
    return mixed, weight_grad[None]


def solution(mesh):
    placed = (
        P(("expert", "fsdp", "dp"), None),
        P(("expert", "fsdp", "dp"), None),
        P(("expert", "fsdp", "dp"), None, None),
        P(("expert", "fsdp", "dp"), None, None),
        P("expert", "fsdp", None),
        P("expert", "fsdp", None),
    )
    sizes = (mesh.shape["expert"] // 2, mesh.shape["dp"] // 2, mesh.shape["fsdp"])
    return jax.shard_map(
        functools.partial(body, *sizes),
        mesh=mesh,
        in_specs=placed,
        out_specs=(P(("expert", "fsdp", "dp"), None), P("expert", ("fsdp", "dp"), None)),
        check_vma=False,
    )
```

time: 175 us -> 161 us (0.920)
  the two profiles are of different devices: /device:TPU:129 before, /device:TPU:103 now
where the time goes in v2:
time: 161 us
  Pallas kernels  157 us (98%)
  local copies, waits for them, and re-layouts  3.91 us (2%)
    pallas_call x1, Pallas kernels, body(): pl.pallas_call(functools.partial(layer_kernel, (zl_n, x_n, y_n)), out_sha...  157 us
    unnamed x2, local copies, waits for them, and re-layouts  3.91 us

profile of v2, /device:TPU:103, one launch (start us, length us, event | category | flops | bytes accessed | tf_op | source)
XLA Modules:
  0.0 161.1 jit_solution(17518695898869561627)
XLA Ops:
  0.6 156.6 %shard_map.77 = (bf16[128,1664]{1,0:T(8,128)(2,1)}, f32[128,1664]{1,0:T(8,128)}) custom-call(s32[2,32]{1,0:T(2,128)} %bitcast.12, f32[2,32]{1,0:T(2,128)} %bitcast.13, bf16[128,1664]{1,0:T(8,128)(2,1)} %tokens.1, bf16[128,1664]{1,0:T(8,128)(2,1)} %grad_out.1, bf16[1024,1664]{1,0:T(8,128)(2,1)} %bitcast.9, bf16[1024,1664]{1,0:T(8,128)(2,1)} %bitcast.10), custom_call_target="tpu_custom_call" | custom-call | tf_op jit(solution)/shard_map/pallas_call | solution.py:415
  157.2 1.8 %copy.10 = bf16[128,1664]{1,0:T(8,128)(2,1)} copy(bf16[128,1664]{1,0:T(8,128)(2,1)} %get-tuple-element.8) | data formatting | bytes 851968
  159.0 2.1 %copy.11 = f32[1,128,1664]{2,1,0:T(8,128)} copy(f32[1,128,1664]{2,1,0:T(8,128)} %bitcast.11) | data formatting | bytes 1703936
